TPU v7x, 32 devices: a whole 2x2x4 slice. The times are simulated.
32 devices in a mesh: slot: 2 (over x), tile: 16 (over z, y, core).
Axes of the slice: x: 2, y: 2, z: 4, core: 2. Of those that a mesh axis runs over, the one named last changes fastest.
Arguments:
- control: float32 [2, 4, 2, 256, 512], P('slot', None, None, 'tile'), may hold values from -28 to 28
- background: bfloat16 [4, 2, 256, 512], P(None, None, 'tile'), may hold values from -6 to 6
- self_weight: bfloat16 [512, 512], replicated, may hold values from -0.25 to 0.25
- neighbour_weight: bfloat16 [512, 512], replicated, may hold values from -0.25 to 0.25
- output_weight: bfloat16 [512, 512], replicated, may hold values from -0.25 to 0.25
- norm_gain: float32 [512], replicated, may hold values from 0.1 to 1.9
- readout: bfloat16 [512, 128], replicated, may hold values from -0.25 to 0.25
- error_weight: float32 [512], replicated, may hold values from 0.3 to 3
- report_owner: int32 [2, 2, 512, 1], P('slot', None, 'tile'), may hold values from 0 to 15, as said below
- report_stencil: int32 [2, 2, 512, 4], P('slot', None, 'tile'), may hold values from 0 to 31
- report_weights: bfloat16 [2, 2, 512, 4], P('slot', None, 'tile'), may hold values from 0.049804688 to 1
- report_values: bfloat16 [2, 2, 512, 128], P('slot', None, 'tile'), may hold values from -6 to 6
- report_precision: bfloat16 [2, 2, 512], P('slot', None, 'tile'), may hold values from 0.049804688 to 0.5
Outputs:
- gradient: float32 [2, 4, 2, 256, 512], P('slot', None, None, 'tile')
Inputs may be any that keep to these rules, and one draw needn't show every extreme that they name: `report_owner`: within the rows of one device for one slot and step (aligned blocks of 32 rows) no owner tile is named more than 5 times; in every slot and step one owner tile is named exactly 5 times by every device of the slot. `report_stencil`: A cell of the owner tile, numbered latitude row * 16 + column within the tile.
All inputs are finite; a program needn't handle non-finite values.
Results may differ from a plain program's by a relative error of at most 0.006.
Values may be sent and summed in bfloat16 or wider, within the bound.
No kernel may reach another device: no remote copies, remote signals or barrier semaphores. Data moves between devices by JAX's collectives and lax.ppermute only.
A program may use at most 64 MiB of HBM per device.

v0:
```python
import functools
import jax
import jax.numpy as jnp
from jax import lax
from jax.experimental import pallas as pl
from jax.experimental.pallas import tpu as pltpu
from jax.sharding import PartitionSpec as P

EPSILON = 1e-06
F32 = jnp.float32
BF16 = jnp.bfloat16
LANES = 128
CAP = 5
SLOTS = 4 * CAP
CHUNK = 32
META = 16
SENDERS = LANES // SLOTS
WIDE = 40
SLIM = 24
VMEM_LIMIT = 28 * 1024 * 1024


def dot(a, b):
    return jnp.dot(a, b, preferred_element_type=F32)


def dot_t(a, b):
    return lax.dot_general(a, b, (((1,), (1,)), ((), ())), preferred_element_type=F32)


def sublane(shape):
    return lax.broadcasted_iota(jnp.int32, shape, 0)


def inverse_rms(x):
    return lax.rsqrt(jnp.mean(x * x, axis=-1, keepdims=True) + EPSILON)


def sigmoid(p):
    return 0.5 * jnp.tanh(0.5 * p) + 0.5


def neighbours(rows):
    width = rows[0].shape[0]
    return [
        0.25 * (rows[1 - i] + pltpu.roll(rows[i], 1, 0) + pltpu.roll(rows[i], width - 1, 0))
        for i in range(2)
    ]


def forward_step(u, n, mean, act, pre, d, gain, ws, wn, wo, width, members, out, fetch=None):
    both = 2 * width
    for m in range(members):
        base = m * both
        rows = []
        for lat in range(2):
            x = u[base + lat * width : base + (lat + 1) * width]
            rows.append((x * inverse_rms(x) * gain).astype(BF16).astype(F32))
        n[base : base + both] = jnp.concatenate(rows, axis=0).astype(BF16)
        mean[base : base + both] = jnp.concatenate(neighbours(rows), axis=0).astype(BF16)
    pre[...] = dot(n[...], ws[...]) + dot(mean[...], wn[...])
    for m in range(members):
        base = m * both
        p = pre[base : base + both]
        sig = sigmoid(p)
        act[base : base + both] = (p * sig).astype(BF16)
        if d is not None:
            pre[base : base + both] = sig * (1.0 + p * (1.0 - sig))
    if d is not None:
        for m in range(members):
            slim_copy(d, pre, m)
    if fetch is not None:
        fetch.wait()
    pre[...] = dot(act[...], wo[...])
    for r in range(2 * members):
        out(r, u[r * width : (r + 1) * width] + pre[r * width : (r + 1) * width])


def slim_edge(wide, r):
    low = wide[r * WIDE + 16 : r * WIDE + 24]
    high = wide[r * WIDE + 32 : r * WIDE + 40]
    return jnp.where(sublane(low.shape) < 4, low, high)


def slim_copy(to, wide, m):
    parts = []
    for r in (2 * m, 2 * m + 1):
        parts += [wide[r * WIDE : r * WIDE + 16], slim_edge(wide, r)]
    both = jnp.concatenate(parts, axis=0)
    to[m * 2 * SLIM : (m + 1) * 2 * SLIM] = both.astype(to.dtype)


def first_kernel(
    control_hbm, owner_hbm, stencil_hbm, weights_hbm, precision_hbm, values_hbm,
    ws_hbm, wn_hbm, readout_hbm, gain_hbm,
    held, out_hbm, ws, wn, readout, gain,
    owner, stencil, weights, precision, values, key, meta, picked, out, sems,
):
    pairs = (
        (owner_hbm, owner), (stencil_hbm, stencil), (weights_hbm, weights),
        (precision_hbm, precision), (values_hbm, values), (control_hbm, held),
        (gain_hbm, gain), (ws_hbm, ws), (wn_hbm, wn), (readout_hbm, readout),
    )
    copies = [pltpu.make_async_copy(source, to, sems.at[i]) for i, (source, to) in enumerate(pairs)]
    for copy in copies:
        copy.start()
    for copy in copies[:5]:
        copy.wait()
    pack(owner, stencil, weights, precision, values, out, key, meta, picked)
    store = pltpu.make_async_copy(out, out_hbm, sems.at[len(pairs)])
    store.start()
    for copy in copies[5:]:
        copy.wait()
    store.wait()


def pack(owner, stencil, weights, precision, values, out, key, meta, picked):
    steps, _, rows = owner.shape
    tiles = out.shape[0] // CHUNK
    total = steps * rows
    place = lax.axis_index("tile") % SENDERS * SLOTS
    earlier = lax.broadcasted_iota(jnp.int32, (rows, rows), 0) < lax.broadcasted_iota(jnp.int32, (rows, rows), 1)
    earlier = earlier.astype(F32).astype(BF16)
    meta[...] = jnp.zeros_like(meta)
    for k in range(steps):
        at = slice(k * rows, (k + 1) * rows)
        named = lax.broadcasted_iota(jnp.int32, (tiles, rows), 0) == owner[k]
        hits = named.astype(F32)
        before = dot(hits.astype(BF16), earlier)
        rank = jnp.sum(hits * before, axis=0, keepdims=True).astype(jnp.int32)
        key[0:1, at] = owner[k] * (2 * CAP) + k * CAP + rank
        meta[4:8, at] = stencil[k].astype(F32)
        meta[8:12, at] = weights[k].astype(F32)
        meta[12:13, at] = precision[k : k + 1].astype(F32)
    row = lax.broadcasted_iota(jnp.int32, (tiles * CHUNK, total), 0)
    tile = row // CHUNK
    slot = row % CHUNK
    other = jnp.where(tile % 2 == 0, (tile + tiles - 1) % tiles, (tile + 1) % tiles)
    mine = slot < 2 * CAP
    wanted = jnp.where(mine, tile * (2 * CAP) + slot, other * (2 * CAP) + slot - 2 * CAP)
    wanted = jnp.where(slot < SLOTS, wanted, -1)
    placement = (wanted == key[...]).astype(F32).astype(BF16)
    picked[...] = dot(placement, values[...])
    entries = dot_t(meta[...].astype(BF16), placement)
    lane = lax.broadcasted_iota(jnp.int32, (META, LANES), 1)
    used = jnp.logical_and(lane >= place, lane < place + SLOTS)
    per_tile = LANES // CHUNK
    for t in range(tiles):
        block = entries[:, t // per_tile * LANES : (t // per_tile + 1) * LANES]
        shift = (place + LANES - t % per_tile * CHUNK) % LANES
        block = jnp.where(used, pltpu.roll(block, shift, 1), 0.0)
        low = picked[t * CHUNK + 16 : (t + 1) * CHUNK]
        picked[t * CHUNK + 16 : (t + 1) * CHUNK] = jnp.where(sublane((META, 1)) < 4, low, block)
    out[...] = picked[...].astype(BF16)


def tile_kernel(control, mate, out, held):
    even = lax.rem(lax.axis_index("tile"), 2) == 0
    size = control.shape[0]
    out[0:size] = control[...].astype(BF16)
    for r in range(size // 16):
        held[r * 2 : (r + 1) * 2] = jnp.where(
            even, mate[r * 16 : r * 16 + 2], mate[r * 16 + 14 : (r + 1) * 16]
        )
    out[size:] = held[...].astype(BF16)


def after_kernel(block, earlier, out):
    out[...] = block[...]


def relay_kernel(control, mate, oth_inner, oth_ends, out, oth, wide):
    tile = lax.axis_index("tile")
    end = jnp.logical_or(tile == 0, tile == lax.axis_size("tile") - 1)
    even = lax.rem(lax.axis_index("tile"), 2) == 0
    size = control.shape[0]
    edge = size // 8
    out[0:size] = control[...]
    wide[...] = jnp.where(end, oth_ends[...].astype(F32), oth_inner[...].astype(F32))
    oth[...] = wide[...].astype(BF16)
    for r in range(size // 16):
        a, b = r * 16, (r + 1) * 16
        out[size + r * 2 : size + (r + 1) * 2] = jnp.where(even, wide[b - 2 : b], wide[a : a + 2])
        start = size + edge + r * 2
        out[start : start + 2] = jnp.where(even, mate[a : a + 2], mate[b - 2 : b])


def forward_kernel(
    wo_hbm, control, mate, oth, ws, wn, gain, readout,
    edge0, u1x, d0x, d1x, f2x, field, final,
    ua, ub, n, mean, act, pre, edge, states, wo, sem,
):
    fetch = pltpu.make_async_copy(wo_hbm, wo, sem)
    fetch.start()
    members = control.shape[0] // 32
    even = lax.rem(lax.axis_index("tile"), 2) == 0
    tile_at = jnp.where(even, 24, 16)
    edge_at = jnp.where(even, 16, 32)
    far = oth[members * 32 :].astype(F32)
    for r in range(2 * members):
        ua[r * WIDE : r * WIDE + 16] = control[r * 16 : (r + 1) * 16]
        ua[pl.ds(pl.multiple_of(r * WIDE + tile_at, 8), 16)] = oth[r * 16 : (r + 1) * 16].astype(F32)
        near4 = jnp.where(even, mate[r * 16 : r * 16 + 4], mate[r * 16 + 12 : (r + 1) * 16])
        far2 = far[r * 2 : (r + 1) * 2]
        edge[...] = jnp.zeros_like(edge)
        edge[0:4] = near4
        edge[6:8] = far2
        edge[8:10] = far2
        edge[12:16] = near4
        ua[pl.ds(pl.multiple_of(r * WIDE + edge_at, 8), 8)] = jnp.where(even, edge[0:8], edge[8:16])
    for r in range(2 * members):
        edge0[r * 8 : (r + 1) * 8] = slim_edge(ua, r)
    g = gain[...]

    def keep(ref):
        def store(r, value):
            ref[r * WIDE : (r + 1) * WIDE] = value

        return store

    def keep_states(ref, k):
        own = k * members * 32
        away = (2 + k) * members * 32
        for r in range(2 * members):
            states[own + r * 16 : own + (r + 1) * 16] = ref[r * WIDE : r * WIDE + 16].astype(BF16)
            taken = ref[pl.ds(pl.multiple_of(r * WIDE + tile_at, 8), 16)]
            states[away + r * 16 : away + (r + 1) * 16] = taken.astype(BF16)

    forward_step(ua, n, mean, act, pre, d0x, g, ws, wn, wo, WIDE, members, keep(ub), fetch)
    for m in range(members):
        slim_copy(u1x, ub, m)
    keep_states(ub, 0)
    forward_step(ub, n, mean, act, pre, d1x, g, ws, wn, wo, WIDE, members, keep(ua))
    for m in range(members):
        slim_copy(f2x, ua, m)
    keep_states(ua, 1)
    final[...] = states[members * 32 : 2 * members * 32]
    read = dot(states[...], readout[...])
    for q in range(4):
        for m in range(members):
            start = (q * members + m) * 32
            field[q * 32 : (q + 1) * 32, m * LANES : (m + 1) * LANES] = read[start : start + 32]


def split(x):
    high = x.astype(BF16)
    return high, (x - high.astype(F32)).astype(BF16)


def observe_kernel(
    tiles,
    ws_hbm, wn_hbm, wo_hbm, readout_hbm, gain_hbm, error_hbm, control_hbm, background_hbm, arrived, field,
    pull1, pull2, message, ws, wn, wo, readout, gain, error, control, background,
    th, tl, ph, plo, vals, spread, wide, sems,
):
    pairs = (
        (readout_hbm, readout), (gain_hbm, gain), (error_hbm, error), (wo_hbm, wo), (wn_hbm, wn), (ws_hbm, ws),
        (control_hbm, control), (background_hbm, background),
    )
    copies = [pltpu.make_async_copy(source, to, sems.at[i]) for i, (source, to) in enumerate(pairs)]
    for copy in copies:
        copy.start()
    steps = 2
    members = field.shape[1] // LANES
    even = lax.rem(lax.axis_index("tile"), 2) == 0
    cells = sublane((32, LANES)).astype(F32)
    lane = lax.broadcasted_iota(jnp.int32, (1, LANES), 1)
    table_of = jnp.where(lane < SENDERS * SLOTS, lane % SLOTS // CAP, -1)
    wide[...] = arrived[...].astype(F32)
    vals[...] = jnp.zeros_like(vals)
    for p in range(th.shape[1] // LANES):
        meta = jnp.zeros((META, LANES), F32)
        for d in range(p * SENDERS, min((p + 1) * SENDERS, tiles)):
            meta += wide[d * CHUNK + 16 : (d + 1) * CHUNK]
            start = p * LANES + d % SENDERS * SLOTS
            vals[start : start + SLOTS] = wide[d * CHUNK : d * CHUNK + SLOTS]
        weight = jnp.zeros((32, LANES), F32)
        for i in range(4):
            weight += jnp.where(cells == meta[4 + i : 5 + i], meta[8 + i : 9 + i], 0.0)
        scaled = weight * meta[12:13]
        wh, wl = split(weight)
        sh, sl = split(scaled)
        parts = ((th, wh.astype(F32)), (tl, wl.astype(F32)), (ph, sh.astype(F32)), (plo, sl.astype(F32)))
        for q in range(2 * steps):
            hit = table_of == q
            for ref, value in parts:
                kept = jnp.where(hit, value, 0.0).astype(BF16)
                ref[q * 32 : (q + 1) * 32, p * LANES : (p + 1) * LANES] = kept
    cross = dot_t(ph[...], th[...]) + dot_t(plo[...], th[...]) + dot_t(ph[...], tl[...])
    taken = vals[...].astype(BF16)
    target = dot(ph[...], taken) + dot(plo[...], taken)
    ch, cl = split(cross)
    fh, fl = split(field[...])
    mixed = dot(ch, fh) + dot(cl, fh) + dot(ch, fl)
    for q in range(2 * steps):
        for m in range(members):
            start = (q * members + m) * 32
            value = mixed[q * 32 : (q + 1) * 32, m * LANES : (m + 1) * LANES] - target[q * 32 : (q + 1) * 32]
            spread[start : start + 32] = value.astype(BF16)
    copies[0].wait()
    pulled = dot_t(spread[...], readout[...])
    size = members * 32
    row8 = sublane((8, 1))
    for k, out in enumerate((pull1, pull2)):
        own = k * size
        away = (2 + k) * size
        for r in range(2 * members):
            out[r * SLIM : r * SLIM + 16] = pulled[own + r * 16 : own + (r + 1) * 16]
            low = pulled[away + r * 16 : away + r * 16 + 8]
            high = pulled[away + r * 16 + 8 : away + r * 16 + 16]
            group = jnp.where(
                even, jnp.where(row8 >= 4, high, 0.0), jnp.where(row8 < 4, low, 0.0)
            )
            out[r * SLIM + 16 : r * SLIM + 24] = group
        for r in range(2 * members):
            pair = spread[own + r * 16 : own + (r + 1) * 16].astype(F32)
            near = jnp.where(even, pair[8:16], pair[0:8])
            message[k * size // 2 + r * 8 : k * size // 2 + (r + 1) * 8] = near
    for copy in copies[1:]:
        copy.wait()


def adjoint_step(u, cot, gb, gm, flat, d, add, out, gain, ws, wn, wo, members):
    both = 2 * SLIM
    gb[...] = cot[...].astype(BF16)
    flat[...] = dot_t(gb[...], wo[...])
    gb[...] = (flat[...] * d[...]).astype(BF16)
    gm[...] = dot_t(gb[...], wn[...])
    flat[...] = dot_t(gb[...], ws[...])
    for m in range(members):
        base = m * both
        rows = []
        for lat in range(2):
            start = base + lat * SLIM
            rows.append(gm[start : start + SLIM].astype(BF16).astype(F32))
        around = neighbours(rows)
        for lat in range(2):
            start = base + lat * SLIM
            x = u[start : start + SLIM]
            s = inverse_rms(x)
            scaled = gain * (flat[start : start + SLIM] + around[lat])
            inner = jnp.mean(x * scaled, axis=-1, keepdims=True)
            value = cot[start : start + SLIM] + s * scaled - x * (s * s * s * inner)
            if add is not None:
                value = value + add[start : start + SLIM]
            out[start : start + SLIM] = value


def edges(nxt, size, edge, r):
    even = lax.rem(lax.axis_index("tile"), 2) == 0
    start = size + r * 2
    far = nxt[start : start + 2]
    start = size + size // 8 + r * 2
    near = nxt[start : start + 2]
    edge[...] = jnp.zeros_like(edge)
    edge[0:2] = near
    edge[6:8] = far
    edge[8:10] = far
    edge[14:16] = near
    return jnp.where(even, edge[0:8], edge[8:16])


def backward_kernel(
    control, edge0, u1x, d0x, d1x, f2x, pull1, pull2, message,
    nxt, ws, wn, wo, gain, error, readout,
    result,
    cot, cot2, extra, gb, gm, flat, mate_pull, edge, u0x, final,
):
    size = control.shape[0]
    members = size // 32
    even = lax.rem(lax.axis_index("tile"), 2) == 0
    slot = lax.axis_index("slot")
    later = jnp.where(slot == lax.axis_size("slot") - 1, 0.0, 1.0)
    gain = gain[...]
    weight = later * error[...]
    row8 = sublane((8, 1))
    mate_pull[...] = dot_t(message[...].astype(BF16), readout[...])
    mate_side = jnp.where(even, 1, 0) == jnp.where(row8 < 4, 1, 0)
    final[...] = f2x[...].astype(F32)
    for r in range(2 * members):
        a, b = r * SLIM, r * SLIM + 16
        cot[a:b] = pull2[a:b] - weight * (nxt[r * 16 : (r + 1) * 16] - final[a:b])
        c, e = b, b + 8
        start = size // 2 + r * 8
        pulled = pull2[c:e] + jnp.where(mate_side, mate_pull[start : start + 8], 0.0)
        cot[c:e] = pulled - weight * (edges(nxt, size, edge, r) - final[c:e])
        extra[a:b] = pull1[a:b]
        extra[c:e] = pull1[c:e] + jnp.where(mate_side, mate_pull[r * 8 : (r + 1) * 8], 0.0)
    adjoint_step(u1x, cot, gb, gm, flat, d1x, extra, cot2, gain, ws, wn, wo, members)
    for r in range(2 * members):
        u0x[r * SLIM : r * SLIM + 16] = control[r * 16 : (r + 1) * 16]
        u0x[r * SLIM + 16 : (r + 1) * SLIM] = edge0[r * 8 : (r + 1) * 8]
    adjoint_step(u0x, cot2, gb, gm, flat, d0x, None, cot, gain, ws, wn, wo, members)
    for r in range(2 * members):
        a, b = r * 16, (r + 1) * 16
        result[a:b] = cot[r * SLIM : r * SLIM + 16] + error[...] * control[a:b]


def last_kernel(base, background, before, error, result):
    first = lax.axis_index("slot") == 0
    taken = jnp.where(first, background[...].astype(F32), before[...].astype(F32))
    result[...] = base[...] - error[...] * taken


def kernel_call(body, outs, scratch, flops, moved, hbm=0, out_places=None):
    def call(*operands):
        operands = [pltpu.with_memory_space_constraint(x, pltpu.HBM) for x in operands[:hbm]] + list(operands[hbm:])
        places = [pltpu.HBM] * hbm + [pltpu.VMEM] * (len(operands) - hbm)
        given = {} if out_places is None else {"out_specs": [pl.BlockSpec(memory_space=p) for p in out_places]}
        return pl.pallas_call(
            body,
            out_shape=outs,
            in_specs=[pl.BlockSpec(memory_space=place) for place in places],
            **given,
            scratch_shapes=scratch,
            compiler_params=pltpu.CompilerParams(vmem_limit_bytes=VMEM_LIMIT),
            cost_estimate=pl.CostEstimate(flops=flops, bytes_accessed=moved, transcendentals=0),
        )(*operands)

    return call


def per_device(
    control,
    background,
    self_weight,
    neighbour_weight,
    output_weight,
    norm_gain,
    readout,
    error_weight,
    report_owner,
    report_stencil,
    report_weights,
    report_values,
    report_precision,
):
    tiles = lax.axis_size("tile")
    slots = lax.axis_size("slot")
    members, lats, cols, channels = control.shape[1:]
    groups = members * lats
    size = groups * cols
    steps = report_owner.shape[1]
    rows = report_owner.shape[2]
    gain = norm_gain.reshape(1, channels)
    error = error_weight.reshape(1, channels)
    flat = control.reshape(size, channels)

    def spec(count, dtype=F32, width=channels):
        return jax.ShapeDtypeStruct((count, width), dtype)

    def scratch(count, dtype=F32, width=channels):
        return pltpu.VMEM((count, width), dtype)

    mate_of = [(i, i ^ 1) for i in range(tiles)]
    other_of = [(i, (i - 1) % tiles if i % 2 == 0 else (i + 1) % tiles) for i in range(tiles)]

    def across(block, shift, route):
        pairs = [
            (((s + shift) % slots) * tiles + i, s * tiles + j)
            for s in range(slots)
            for i, j in route
        ]
        return lax.ppermute(block, ("slot", "tile"), pairs)

    straight = [(i, i) for i in range(tiles)]
    mate = lax.ppermute(flat, "tile", mate_of)
    held, packed, ws, wn, readout_first, gain_first = kernel_call(
        first_kernel,
        [spec(size), spec(tiles * CHUNK, BF16, LANES), spec(channels, BF16), spec(channels, BF16)]
        + [spec(channels, BF16, LANES), spec(1)],
        [
            pltpu.VMEM((steps, 1, rows), jnp.int32),
            pltpu.VMEM((steps, 4, rows), jnp.int32),
            pltpu.VMEM((steps, 4, rows), BF16),
            pltpu.VMEM((steps, rows), BF16),
            scratch(steps * rows, BF16, LANES),
            pltpu.VMEM((1, steps * rows), jnp.int32),
            scratch(META, F32, steps * rows),
            scratch(tiles * CHUNK, F32, LANES),
            scratch(tiles * CHUNK, BF16, LANES),
            pltpu.SemaphoreType.DMA((11,)),
        ],
        10**7,
        200000,
        hbm=10,
        out_places=[pltpu.VMEM, pltpu.HBM] + [pltpu.VMEM] * 4,
    )(
        flat,
        jnp.transpose(report_owner[0], (0, 2, 1)),
        jnp.transpose(report_stencil[0], (0, 2, 1)),
        jnp.transpose(report_weights[0], (0, 2, 1)),
        report_precision[0],
        report_values[0].reshape(steps * rows, LANES),
        self_weight,
        neighbour_weight,
        readout,
        gain,
    )
    sent = kernel_call(
        tile_kernel, spec(groups * (cols + 2), BF16), [scratch(groups * 2)], 1000, 400000
    )(held, mate)
    ends = (0, tiles - 1)
    oth_inner = lax.ppermute(sent, "tile", [(i, i if i in ends else j) for i, j in other_of])
    again = kernel_call(after_kernel, spec(groups * (cols + 2), BF16), [], 10**11, 300000)(sent, oth_inner)
    oth_ends = lax.ppermute(again, "tile", [(i, j if i in ends else i) for i, j in other_of])
    arrived = lax.all_to_all(packed, "tile", split_axis=0, concat_axis=0, tiled=True)

    message, oth = kernel_call(
        relay_kernel,
        [spec(size + 4 * groups), spec(groups * (cols + 2), BF16)],
        [scratch(groups * (cols + 2))],
        1000,
        700000,
    )(held, mate, oth_inner, oth_ends)
    nxt = across(message, 1, straight)
    wide = groups * WIDE
    slim = groups * SLIM
    edge0, u1x, d0x, d1x, f2x, field, final = kernel_call(
        forward_kernel,
        [spec(groups * 8), spec(slim)] + [spec(slim, BF16)] * 3
        + [spec(4 * lats * cols, F32, members * LANES), spec(size, BF16)],
        [scratch(wide), scratch(wide), scratch(wide, BF16), scratch(wide, BF16), scratch(wide, BF16)]
        + [scratch(wide), scratch(16), scratch(4 * size, BF16)]
        + [scratch(channels, BF16), pltpu.SemaphoreType.DMA],
        12 * wide * channels * channels,
        4000000,
        hbm=1,
    )(output_weight, held, mate, oth, ws, wn, gain_first, readout_first)
    before = across(final, -1, straight)
    total = -(-tiles // SENDERS) * LANES
    handed = [self_weight, neighbour_weight, output_weight, readout, gain, error]
    handed += [flat, background.reshape(size, channels)]
    pull1, pull2, message, *handed = kernel_call(
        functools.partial(observe_kernel, tiles),
        [spec(slim), spec(slim), spec(size, F32, LANES)]
        + [jax.ShapeDtypeStruct(block.shape, block.dtype) for block in handed],
        [scratch(128, BF16, total)] * 4
        + [scratch(total, F32, LANES), scratch(4 * size, BF16, LANES), scratch(tiles * CHUNK, F32, LANES)]
        + [pltpu.SemaphoreType.DMA((8,))],
        10**9,
        2000000,
        hbm=8,
    )(*handed, arrived, field)
    ws, wn, wo, readout, gain, error, held, background = handed
    from_mate = lax.ppermute(message, "tile", mate_of)
    base = kernel_call(
        backward_kernel,
        spec(size),
        [scratch(slim), scratch(slim), scratch(slim), scratch(slim, BF16), scratch(slim), scratch(slim)]
        + [scratch(size), scratch(16), scratch(slim), scratch(slim)],
        12 * slim * channels * channels,
        6000000,
    )(held, edge0, u1x, d0x, d1x, f2x, pull1, pull2, from_mate, nxt, ws, wn, wo, gain, error, readout)
    result = kernel_call(last_kernel, spec(size), [], 10**6, 900000)(base, background, before, error)
    return result.reshape(control.shape)


def solution(mesh):
    in_specs = (
        P("slot", None, None, "tile", None),
        P(None, None, "tile", None),
        P(),
        P(),
        P(),
        P(),
        P(),
        P(),
        P("slot", None, "tile", None),
        P("slot", None, "tile", None),
        P("slot", None, "tile", None),
        P("slot", None, "tile", None),
        P("slot", None, "tile"),
    )
    out_specs = P("slot", None, None, "tile", None)
    return jax.shard_map(
        per_device, mesh=mesh, in_specs=in_specs, out_specs=out_specs, check_vma=False
    )
```

profile of v0, /device:TPU:0, one launch (start us, length us, event | category | flops | bytes accessed | tf_op | source)
XLA Modules:
  0.0 32.4 jit_solution(8985731071564291195)
XLA Ops:
  0.0 0.5 %collective-permute-start = (f32[128,512]{1,0:T(8,128)}, f32[128,512]{1,0:T(8,128)S(1)}, u32[]{:S(2)}, u32[]{:S(2)}) collective-permute-start(f32[128,512]{1,0:T(8,128)} %bitcast.19), channel_id=1, source_target_pairs={{0,1},{1,0},{2,3},{3,2},{4,5},{5,4},{6,7},{7,6},{8,9},{9,8},{10,11... | collective-permute-start | bytes 786440 | tf_op jit(solution)/shard_map/ppermute | solution.py:467
  0.5 2.0 %shard_map.127 = (f32[128,512]{1,0:T(8,128)S(1)}, bf16[512,128]{1,0:T(8,128)(2,1)}, bf16[512,512]{1,0:T(8,128)(2,1)S(1)}, bf16[512,512]{1,0:T(8,128)(2,1)S(1)}, ...) custom-call(f32[128,512]{1,0:T(8,128)} %bitcast.20, s32[2,1,32]{2,1,0:T(1,128)} %bitcast.27, s32[2,4,32]{2,1,0:T(4,128)} %bitcast.23, ...), custom_call_target="tpu_custom_call" | custom-call | flops 10000000 | bytes 200000 | tf_op jit(solution)/shard_map/pallas_call | solution.py:410
  2.5 0.0 copy-start
  2.5 0.0 collective-permute-done.mate
  2.5 0.6 %copy-done = bf16[512,128]{1,0:T(8,128)(2,1)} copy-done((bf16[512,128]{1,0:T(8,128)(2,1)}, bf16[512,128]{1,0:T(8,128)(2,1)S(1)}, u32[]{:S(2)}) %copy-start) | copy-done | bytes 131096
  3.1 0.7 %collective-permute-start.1 = (bf16[144,512]{1,0:T(8,128)(2,1)S(1)}, bf16[144,512]{1,0:T(8,128)(2,1)S(1)}, u32[]{:S(2)}, u32[]{:S(2)}) collective-permute-start(bf16[144,512]{1,0:T(8,128)(2,1)S(1)} %shard_map.128.block), channel_id=1, source_target_pairs={{0,0},{1,2},{2,1},{3,4},{4,3},{5,6},{6,5},{7,8},{8,7},{9,10},{10,9... | collective-permute-start | bytes 442376 | tf_op jit(solution)/shard_map/ppermute | solution.py:504
  3.8 0.0 collective-permute-done.1.earlier.oth_inner
  3.8 7.6 %collective-permute-start.2 = (bf16[144,512]{1,0:T(8,128)(2,1)S(1)}, bf16[144,512]{1,0:T(8,128)(2,1)S(1)}, u32[]{:S(2)}, u32[]{:S(2)}) collective-permute-start(bf16[144,512]{1,0:T(8,128)(2,1)S(1)} %shard_map.129), channel_id=1, source_target_pairs={{0,15},{1,1},{2,2},{3,3},{4,4},{5,5},{6,6},{7,7},{8,8},{9,9},{10,1... | collective-permute-start | bytes 442376 | tf_op jit(solution)/shard_map/ppermute | solution.py:506
  11.4 6.5 %all-to-all-start = ((bf16[16,32,128]{2,1,0:T(8,128)(2,1)}), bf16[16,32,128]{2,1,0:T(8,128)(2,1)S(1)}, u32[]{:S(2)}, u32[]{:S(2)}) async-start(bf16[16,32,128]{2,1,0:T(8,128)(2,1)} %bitcast.12), calls=%async_computation | async-start | bytes 262144 | tf_op jit(solution)/shard_map/all_to_all | solution.py:507
  18.0 0.0 copy-start.1
  18.0 0.0 collective-permute-done.2.oth_ends
  18.0 0.1 shard_map.130
  18.1 1.6 %collective-permute-start.4 = (f32[160,512]{1,0:T(8,128)S(1)}, f32[160,512]{1,0:T(8,128)S(1)}, u32[]{:S(2)}, u32[]{:S(2)}) collective-permute-start(f32[160,512]{1,0:T(8,128)S(1)} %get-tuple-element.48), channel_id=1, source_target_pairs={{16,0},{17,1},{18,2},{19,3},{20,4},{21,5},{22,6},{23,7},{24,8},{25... | collective-permute-start | bytes 983048 | tf_op jit(solution)/shard_map/ppermute | solution.py:464
  19.7 0.0 copy-done.1
  19.7 3.3 %shard_map.131 = (f32[64,512]{1,0:T(8,128)S(1)}, f32[192,512]{1,0:T(8,128)S(1)}, bf16[192,512]{1,0:T(8,128)(2,1)S(1)}, bf16[192,512]{1,0:T(8,128)(2,1)S(1)}, bf1...) custom-call(bf16[512,512]{1,0:T(8,128)(2,1)} %wo_hbm.3, ...), custom_call_target="tpu_custom_call" | custom-call | flops 1006632960 | bytes 4000000 | tf_op jit(solution)/shard_map/pallas_call | solution.py:410
  23.0 0.0 copy-start.2
  23.0 0.7 %copy-done.2 = f32[128,512]{1,0:T(8,128)} copy-done((f32[128,512]{1,0:T(8,128)}, f32[128,512]{1,0:T(8,128)S(1)}, u32[]{:S(2)}) %copy-start.2) | copy-done | bytes 262168
  23.7 0.7 %collective-permute-start.5 = (bf16[128,512]{1,0:T(8,128)(2,1)}, bf16[128,512]{1,0:T(8,128)(2,1)S(1)}, u32[]{:S(2)}, u32[]{:S(2)}) collective-permute-start(bf16[128,512]{1,0:T(8,128)(2,1)} %get-tuple-element.56), channel_id=1, source_target_pairs={{16,0},{17,1},{18,2},{19,3},{20,4},{21,5},{22,6},{23,7},{24,8},{25... | collective-permute-start | bytes 393224 | tf_op jit(solution)/shard_map/ppermute | solution.py:464
  24.4 1.5 %all-to-all-done = bf16[16,32,128]{2,1,0:T(8,128)(2,1)S(1)} async-done(((bf16[16,32,128]{2,1,0:T(8,128)(2,1)}), bf16[16,32,128]{2,1,0:T(8,128)(2,1)S(1)}, u32[]{:S(2)}, u32[]{:S(2)}) %all-to-all-start) | async-done | bytes 131104 | tf_op jit(solution)/shard_map/all_to_all | solution.py:507
  25.9 0.0 copy-start.3
  25.9 0.9 %copy-done.3 = f32[128,512]{1,0:T(8,128)S(1)} copy-done((f32[128,512]{1,0:T(8,128)S(1)}, f32[128,512]{1,0:T(8,128)}, u32[]{:S(2)}) %copy-start.3) | copy-done | bytes 262168
  26.8 1.7 %shard_map.132 = (f32[192,512]{1,0:T(8,128)S(1)}, f32[192,512]{1,0:T(8,128)S(1)}, f32[128,128]{1,0:T(8,128)S(1)}, bf16[512,512]{1,0:T(8,128)(2,1)S(1)}, bf16[512...) custom-call(bf16[512,512]{1,0:T(8,128)(2,1)} %ws_hbm.3, ...), custom_call_target="tpu_custom_call" | custom-call | flops 1000000000 | bytes 2000000 | tf_op jit(solution)/shard_map/pallas_call | solution.py:410
  28.6 0.1 collective-permute-start.3
  28.7 1.2 %collective-permute-done.3.message = f32[128,128]{1,0:T(8,128)S(1)} collective-permute-done((f32[128,128]{1,0:T(8,128)S(1)}, f32[128,128]{1,0:T(8,128)S(1)}, u32[]{:S(2)}, u32[]{:S(2)}) %collective-permute-start.3) | collective-permute-done | bytes 65568 | tf_op jit(solution)/shard_map/ppermute | solution.py:546
  29.9 0.0 collective-permute-done.4.nxt
  29.9 1.7 %shard_map.133.base = f32[128,512]{1,0:T(8,128)S(1)} custom-call(f32[128,512]{1,0:T(8,128)S(1)} %get-tuple-element.39.control, f32[64,512]{1,0:T(8,128)S(1)} %get-tuple-element.40.edge0, f32[192,512]{1,0:T(8,128)S(1)} %get-tuple-element.41.u1x, bf16[192,512]{1,0:T(8,128)(2,1)S(1)} %get-tuple-element.42.d0x, bf16[192,512]{1,0:T(8,128)(2,1)S(1)} %get-tuple-element.43.d1x, ...), custom_call_target="tpu_custom_call" | custom-call | flops 603979776 | bytes 6000000 | tf_op jit(solution)/shard_map/pallas_call | solution.py:410
  31.6 0.0 collective-permute-done.5.before
  31.6 0.8 %shard_map.134 = f32[128,512]{1,0:T(8,128)} custom-call(f32[128,512]{1,0:T(8,128)S(1)} %shard_map.133.base, bf16[128,512]{1,0:T(8,128)(2,1)S(1)} %get-tuple-element.55.background, bf16[128,512]{1,0:T(8,128)(2,1)S(1)} %collective-permute-done.5.before, f32[1,512]{1,0:T(1,128)S(1)} %get-tuple-element.53.error), custom_call_target="tpu_custom_call" | custom-call | flops 1000000 | bytes 900000 | tf_op jit(solution)/shard_map/pallas_call | solution.py:410
  (2 shorter events, 0.1 us)
Async XLA Ops:
  0.0 2.5 %collective-permute-start = (f32[128,512]{1,0:T(8,128)}, f32[128,512]{1,0:T(8,128)S(1)}, u32[]{:S(2)}, u32[]{:S(2)}) collective-permute-start(f32[128,512]{1,0:T(8,128)} %bitcast.19), channel_id=1, source_target_pairs={{0,1},{1,0},{2,3},{3,2},{4,5},{5,4},{6,7},{7,6},{8,9},{9,8},{10,11... | collective-permute-start | bytes 786440 | tf_op jit(solution)/shard_map/ppermute | solution.py:467
  2.5 0.7 %copy-start = (bf16[512,128]{1,0:T(8,128)(2,1)}, bf16[512,128]{1,0:T(8,128)(2,1)S(1)}, u32[]{:S(2)}) copy-start(bf16[512,128]{1,0:T(8,128)(2,1)S(1)} %get-tuple-element.37.readout) | copy-start | bytes 393220
  3.1 0.7 %collective-permute-start.1 = (bf16[144,512]{1,0:T(8,128)(2,1)S(1)}, bf16[144,512]{1,0:T(8,128)(2,1)S(1)}, u32[]{:S(2)}, u32[]{:S(2)}) collective-permute-start(bf16[144,512]{1,0:T(8,128)(2,1)S(1)} %shard_map.128.block), channel_id=1, source_target_pairs={{0,0},{1,2},{2,1},{3,4},{4,3},{5,6},{6,5},{7,8},{8,7},{9,10},{10,9... | collective-permute-start | bytes 442376 | tf_op jit(solution)/shard_map/ppermute | solution.py:504
  3.8 14.2 %collective-permute-start.2 = (bf16[144,512]{1,0:T(8,128)(2,1)S(1)}, bf16[144,512]{1,0:T(8,128)(2,1)S(1)}, u32[]{:S(2)}, u32[]{:S(2)}) collective-permute-start(bf16[144,512]{1,0:T(8,128)(2,1)S(1)} %shard_map.129), channel_id=1, source_target_pairs={{0,15},{1,1},{2,2},{3,3},{4,4},{5,5},{6,6},{7,7},{8,8},{9,9},{10,1... | collective-permute-start | bytes 442376 | tf_op jit(solution)/shard_map/ppermute | solution.py:506
  11.4 14.5 %all-to-all-start = ((bf16[16,32,128]{2,1,0:T(8,128)(2,1)}), bf16[16,32,128]{2,1,0:T(8,128)(2,1)S(1)}, u32[]{:S(2)}, u32[]{:S(2)}) async-start(bf16[16,32,128]{2,1,0:T(8,128)(2,1)} %bitcast.12), calls=%async_computation | async-start | bytes 262144 | tf_op jit(solution)/shard_map/all_to_all | solution.py:507
  18.0 1.7 %copy-start.1 = (bf16[512,128]{1,0:T(8,128)(2,1)S(1)}, bf16[512,128]{1,0:T(8,128)(2,1)}, u32[]{:S(2)}) copy-start(bf16[512,128]{1,0:T(8,128)(2,1)} %copy-done) | copy-start | bytes 393220
  18.1 11.8 %collective-permute-start.4 = (f32[160,512]{1,0:T(8,128)S(1)}, f32[160,512]{1,0:T(8,128)S(1)}, u32[]{:S(2)}, u32[]{:S(2)}) collective-permute-start(f32[160,512]{1,0:T(8,128)S(1)} %get-tuple-element.48), channel_id=1, source_target_pairs={{16,0},{17,1},{18,2},{19,3},{20,4},{21,5},{22,6},{23,7},{24,8},{25... | collective-permute-start | bytes 983048 | tf_op jit(solution)/shard_map/ppermute | solution.py:464
  23.0 0.7 %copy-start.2 = (f32[128,512]{1,0:T(8,128)}, f32[128,512]{1,0:T(8,128)S(1)}, u32[]{:S(2)}) copy-start(f32[128,512]{1,0:T(8,128)S(1)} %get-tuple-element.38.field) | copy-start | bytes 786436
  23.7 7.9 %collective-permute-start.5 = (bf16[128,512]{1,0:T(8,128)(2,1)}, bf16[128,512]{1,0:T(8,128)(2,1)S(1)}, u32[]{:S(2)}, u32[]{:S(2)}) collective-permute-start(bf16[128,512]{1,0:T(8,128)(2,1)} %get-tuple-element.56), channel_id=1, source_target_pairs={{16,0},{17,1},{18,2},{19,3},{20,4},{21,5},{22,6},{23,7},{24,8},{25... | collective-permute-start | bytes 393224 | tf_op jit(solution)/shard_map/ppermute | solution.py:464
  25.9 1.0 %copy-start.3 = (f32[128,512]{1,0:T(8,128)S(1)}, f32[128,512]{1,0:T(8,128)}, u32[]{:S(2)}) copy-start(f32[128,512]{1,0:T(8,128)} %copy-done.2) | copy-start | bytes 786436
  28.6 1.3 %collective-permute-start.3 = (f32[128,128]{1,0:T(8,128)S(1)}, f32[128,128]{1,0:T(8,128)S(1)}, u32[]{:S(2)}, u32[]{:S(2)}) collective-permute-start(f32[128,128]{1,0:T(8,128)S(1)} %get-tuple-element.47), channel_id=1, source_target_pairs={{0,1},{1,0},{2,3},{3,2},{4,5},{5,4},{6,7},{7,6},{8,9},{9,8},{10,11... | collective-permute-start | bytes 196616 | tf_op jit(solution)/shard_map/ppermute | solution.py:546
where the time goes:
time: 32.7 us; the launch traced here: 32.4 us
  starting transfers between devices  17.6 us (54%)
  Pallas kernels  9.63 us (29%)
  waiting for transfers between devices  2.77 us (8%)
  local copies, waits for them, and re-layouts  2.24 us (7%)
    pallas_call x8, Pallas kernels, call(): pl.pallas_call(body, out_shape=outs, in_specs=[pl.BlockSpec(memory_space=...  9.63 us
    ppermute x1, starting transfers between devices, per_device(): lax.ppermute(again, 'tile', [(i, j if i in ends else i) for i, j in other...  7.58 us
    all_to_all x1, starting transfers between devices, per_device(): lax.all_to_all(packed, 'tile', split_axis=0, concat_axis=0, tiled=True)  6.55 us
    ppermute x2, starting transfers between devices, across(): return lax.ppermute(block, ('slot', 'tile'), pairs)  2.26 us
    unnamed x8, local copies, waits for them, and re-layouts  2.24 us
    all_to_all x1, waiting for transfers between devices, per_device(): lax.all_to_all(packed, 'tile', split_axis=0, concat_axis=0, tiled=True)  1.52 us
    ppermute x1, waiting for transfers between devices, per_device(): from_mate = lax.ppermute(message, 'tile', mate_of)  1.24 us
    ppermute x1, starting transfers between devices, per_device(): lax.ppermute(sent, 'tile', [(i, i if i in ends else j) for i, j in other_...  0.66 us
  transfers between devices with their start and end apart: 7, of which 2 were waited for; matrix products, arithmetic and copies ran while one was open for 0% of the time, Pallas kernels for 27%

commit v1 on v0

--- a/solution.py
+++ b/solution.py
@@ -48,7 +48,7 @@
     ]
 
 
-def forward_step(u, n, mean, act, pre, d, gain, ws, wn, wo, width, members, out, fetch=None):
+def forward_step(u, n, mean, act, pre, d, gain, ws, wn, wo, width, members, out, copies=()):
     both = 2 * width
     for m in range(members):
         base = m * both
@@ -58,6 +58,8 @@
             rows.append((x * inverse_rms(x) * gain).astype(BF16).astype(F32))
         n[base : base + both] = jnp.concatenate(rows, axis=0).astype(BF16)
         mean[base : base + both] = jnp.concatenate(neighbours(rows), axis=0).astype(BF16)
+    for copy in copies[:2]:
+        copy.wait()
     pre[...] = dot(n[...], ws[...]) + dot(mean[...], wn[...])
     for m in range(members):
         base = m * both
@@ -69,8 +71,8 @@
     if d is not None:
         for m in range(members):
             slim_copy(d, pre, m)
-    if fetch is not None:
-        fetch.wait()
+    for copy in copies[2:]:
+        copy.wait()
     pre[...] = dot(act[...], wo[...])
     for r in range(2 * members):
         out(r, u[r * width : (r + 1) * width] + pre[r * width : (r + 1) * width])
@@ -92,14 +94,12 @@
 
 def first_kernel(
     control_hbm, owner_hbm, stencil_hbm, weights_hbm, precision_hbm, values_hbm,
-    ws_hbm, wn_hbm, readout_hbm, gain_hbm,
-    held, out_hbm, ws, wn, readout, gain,
+    held, out_hbm,
     owner, stencil, weights, precision, values, key, meta, picked, out, sems,
 ):
     pairs = (
         (owner_hbm, owner), (stencil_hbm, stencil), (weights_hbm, weights),
         (precision_hbm, precision), (values_hbm, values), (control_hbm, held),
-        (gain_hbm, gain), (ws_hbm, ws), (wn_hbm, wn), (readout_hbm, readout),
     )
     copies = [pltpu.make_async_copy(source, to, sems.at[i]) for i, (source, to) in enumerate(pairs)]
     for copy in copies:
@@ -165,34 +165,30 @@
     out[size:] = held[...].astype(BF16)
 
 
-def after_kernel(block, earlier, out):
-    out[...] = block[...]
-
-
-def relay_kernel(control, mate, oth_inner, oth_ends, out, oth, wide):
-    tile = lax.axis_index("tile")
-    end = jnp.logical_or(tile == 0, tile == lax.axis_size("tile") - 1)
+def relay_kernel(control, mate, oth, out, near4, wide):
     even = lax.rem(lax.axis_index("tile"), 2) == 0
     size = control.shape[0]
     edge = size // 8
     out[0:size] = control[...]
-    wide[...] = jnp.where(end, oth_ends[...].astype(F32), oth_inner[...].astype(F32))
-    oth[...] = wide[...].astype(BF16)
+    wide[...] = oth[0:size].astype(F32)
     for r in range(size // 16):
         a, b = r * 16, (r + 1) * 16
         out[size + r * 2 : size + (r + 1) * 2] = jnp.where(even, wide[b - 2 : b], wide[a : a + 2])
+        near4[r * 4 : (r + 1) * 4] = jnp.where(even, mate[a : a + 4], mate[b - 4 : b])
         start = size + edge + r * 2
         out[start : start + 2] = jnp.where(even, mate[a : a + 2], mate[b - 2 : b])
 
 
 def forward_kernel(
-    wo_hbm, control, mate, oth, ws, wn, gain, readout,
+    gain_hbm, ws_hbm, wn_hbm, wo_hbm, readout_hbm, control, mate, oth,
     edge0, u1x, d0x, d1x, f2x, field, final,
-    ua, ub, n, mean, act, pre, edge, states, wo, sem,
+    ua, ub, n, mean, act, pre, edge, states, gain, ws, wn, wo, readout, sems,
 ):
-    fetch = pltpu.make_async_copy(wo_hbm, wo, sem)
-    fetch.start()
-    members = control.shape[0] // 32
+    pairs = ((gain_hbm, gain), (ws_hbm, ws), (wn_hbm, wn), (wo_hbm, wo), (readout_hbm, readout))
+    copies = [pltpu.make_async_copy(source, to, sems.at[i]) for i, (source, to) in enumerate(pairs)]
+    for copy in copies:
+        copy.start()
+    members = final.shape[0] // 32
     even = lax.rem(lax.axis_index("tile"), 2) == 0
     tile_at = jnp.where(even, 24, 16)
     edge_at = jnp.where(even, 16, 32)
@@ -200,7 +196,7 @@
     for r in range(2 * members):
         ua[r * WIDE : r * WIDE + 16] = control[r * 16 : (r + 1) * 16]
         ua[pl.ds(pl.multiple_of(r * WIDE + tile_at, 8), 16)] = oth[r * 16 : (r + 1) * 16].astype(F32)
-        near4 = jnp.where(even, mate[r * 16 : r * 16 + 4], mate[r * 16 + 12 : (r + 1) * 16])
+        near4 = mate[r * 4 : (r + 1) * 4]
         far2 = far[r * 2 : (r + 1) * 2]
         edge[...] = jnp.zeros_like(edge)
         edge[0:4] = near4
@@ -210,6 +206,7 @@
         ua[pl.ds(pl.multiple_of(r * WIDE + edge_at, 8), 8)] = jnp.where(even, edge[0:8], edge[8:16])
     for r in range(2 * members):
         edge0[r * 8 : (r + 1) * 8] = slim_edge(ua, r)
+    copies[0].wait()
     g = gain[...]
 
     def keep(ref):
@@ -226,7 +223,7 @@
             taken = ref[pl.ds(pl.multiple_of(r * WIDE + tile_at, 8), 16)]
             states[away + r * 16 : away + (r + 1) * 16] = taken.astype(BF16)
 
-    forward_step(ua, n, mean, act, pre, d0x, g, ws, wn, wo, WIDE, members, keep(ub), fetch)
+    forward_step(ua, n, mean, act, pre, d0x, g, ws, wn, wo, WIDE, members, keep(ub), copies[1:])
     for m in range(members):
         slim_copy(u1x, ub, m)
     keep_states(ub, 0)
@@ -465,10 +462,9 @@
 
     straight = [(i, i) for i in range(tiles)]
     mate = lax.ppermute(flat, "tile", mate_of)
-    held, packed, ws, wn, readout_first, gain_first = kernel_call(
+    held, packed = kernel_call(
         first_kernel,
-        [spec(size), spec(tiles * CHUNK, BF16, LANES), spec(channels, BF16), spec(channels, BF16)]
-        + [spec(channels, BF16, LANES), spec(1)],
+        [spec(size), spec(tiles * CHUNK, BF16, LANES)],
         [
             pltpu.VMEM((steps, 1, rows), jnp.int32),
             pltpu.VMEM((steps, 4, rows), jnp.int32),
@@ -479,12 +475,12 @@
             scratch(META, F32, steps * rows),
             scratch(tiles * CHUNK, F32, LANES),
             scratch(tiles * CHUNK, BF16, LANES),
-            pltpu.SemaphoreType.DMA((11,)),
+            pltpu.SemaphoreType.DMA((7,)),
         ],
         10**7,
         200000,
-        hbm=10,
-        out_places=[pltpu.VMEM, pltpu.HBM] + [pltpu.VMEM] * 4,
+        hbm=6,
+        out_places=[pltpu.VMEM, pltpu.HBM],
     )(
         flat,
         jnp.transpose(report_owner[0], (0, 2, 1)),
@@ -492,27 +488,16 @@
         jnp.transpose(report_weights[0], (0, 2, 1)),
         report_precision[0],
         report_values[0].reshape(steps * rows, LANES),
-        self_weight,
-        neighbour_weight,
-        readout,
-        gain,
     )
     sent = kernel_call(
         tile_kernel, spec(groups * (cols + 2), BF16), [scratch(groups * 2)], 1000, 400000
     )(held, mate)
-    ends = (0, tiles - 1)
-    oth_inner = lax.ppermute(sent, "tile", [(i, i if i in ends else j) for i, j in other_of])
-    again = kernel_call(after_kernel, spec(groups * (cols + 2), BF16), [], 10**11, 300000)(sent, oth_inner)
-    oth_ends = lax.ppermute(again, "tile", [(i, j if i in ends else i) for i, j in other_of])
+    oth = lax.ppermute(sent, "tile", other_of)
     arrived = lax.all_to_all(packed, "tile", split_axis=0, concat_axis=0, tiled=True)
 
-    message, oth = kernel_call(
-        relay_kernel,
-        [spec(size + 4 * groups), spec(groups * (cols + 2), BF16)],
-        [scratch(groups * (cols + 2))],
-        1000,
-        700000,
-    )(held, mate, oth_inner, oth_ends)
+    message, near4 = kernel_call(
+        relay_kernel, [spec(size + 4 * groups), spec(4 * groups)], [scratch(size)], 1000, 700000
+    )(held, mate, oth)
     nxt = across(message, 1, straight)
     wide = groups * WIDE
     slim = groups * SLIM
@@ -522,11 +507,12 @@
         + [spec(4 * lats * cols, F32, members * LANES), spec(size, BF16)],
         [scratch(wide), scratch(wide), scratch(wide, BF16), scratch(wide, BF16), scratch(wide, BF16)]
         + [scratch(wide), scratch(16), scratch(4 * size, BF16)]
-        + [scratch(channels, BF16), pltpu.SemaphoreType.DMA],
-        12 * wide * channels * channels,
+        + [scratch(1), scratch(channels, BF16), scratch(channels, BF16), scratch(channels, BF16)]
+        + [scratch(channels, BF16, LANES), pltpu.SemaphoreType.DMA((5,))],
+        10**11,
         4000000,
-        hbm=1,
-    )(output_weight, held, mate, oth, ws, wn, gain_first, readout_first)
+        hbm=5,
+    )(gain, self_weight, neighbour_weight, output_weight, readout, message, near4, oth)
     before = across(final, -1, straight)
     total = -(-tiles // SENDERS) * LANES
     handed = [self_weight, neighbour_weight, output_weight, readout, gain, error]

time: 32.7 us -> 25.7 us (0.79)
  starting transfers between devices: 17.6 us -> 11.9 us
  local copies, waits for them, and re-layouts: 2.24 us -> 0 us
  waiting for transfers between devices: 2.77 us -> 3.7 us
    all_to_all x1, starting transfers between devices: 6.55 us -> 3.51 us  [per_device(): lax.all_to_all(packed, 'tile', split_axis=0, concat_axis=0, tiled=True)]
    ppermute x2 -> x1, starting transfers between devices: 8.23 us -> 5.73 us  [per_device(): oth = lax.ppermute(sent, 'tile', other_of)]
    unnamed x8 -> x0, local copies, waits for them, and re-layouts: 2.24 us -> none
    all_to_all x1, waiting for transfers between devices: 1.52 us -> 2.19 us  [per_device(): lax.all_to_all(packed, 'tile', split_axis=0, concat_axis=0, tiled=True)]
    pallas_call x8 -> x7, Pallas kernels: 9.63 us -> 9.69 us  [call(): pl.pallas_call(body, out_shape=outs, in_specs=[pl.BlockSpec(memory_space=...]
  transfers between devices with their start and end apart: 7 -> 6, of which waited for: 2 -> 3; matrix products, arithmetic and copies ran while one was open for 0% -> 0% of each run, Pallas kernels for 27% -> 35%
where the time goes in v1:
time: 25.7 us; the launch traced here: 25.4 us
  starting transfers between devices  11.9 us (46%)
  Pallas kernels  9.69 us (38%)
  waiting for transfers between devices  3.7 us (14%)
    pallas_call x7, Pallas kernels, call(): pl.pallas_call(body, out_shape=outs, in_specs=[pl.BlockSpec(memory_space=...  9.69 us
    ppermute x1, starting transfers between devices, per_device(): oth = lax.ppermute(sent, 'tile', other_of)  5.73 us
    all_to_all x1, starting transfers between devices, per_device(): lax.all_to_all(packed, 'tile', split_axis=0, concat_axis=0, tiled=True)  3.51 us
    all_to_all x1, waiting for transfers between devices, per_device(): lax.all_to_all(packed, 'tile', split_axis=0, concat_axis=0, tiled=True)  2.19 us
    ppermute x2, starting transfers between devices, across(): return lax.ppermute(block, ('slot', 'tile'), pairs)  2.16 us
    ppermute x1, waiting for transfers between devices, per_device(): from_mate = lax.ppermute(message, 'tile', mate_of)  1.24 us
  transfers between devices with their start and end apart: 6, of which 3 were waited for; matrix products, arithmetic and copies ran while one was open for 0% of the time, Pallas kernels for 35%

profile of v1, /device:TPU:0, one launch (start us, length us, event | category | flops | bytes accessed | tf_op | source)
XLA Modules:
  0.0 25.4 jit_solution(14106884107433208779)
XLA Ops:
  0.0 0.5 %collective-permute-start = (f32[128,512]{1,0:T(8,128)}, f32[128,512]{1,0:T(8,128)S(1)}, u32[]{:S(2)}, u32[]{:S(2)}) collective-permute-start(f32[128,512]{1,0:T(8,128)} %bitcast.19), channel_id=1, source_target_pairs={{0,1},{1,0},{2,3},{3,2},{4,5},{5,4},{6,7},{7,6},{8,9},{9,8},{10,11... | collective-permute-start | bytes 786440 | tf_op jit(solution)/shard_map/ppermute | solution.py:464
  0.5 2.0 %shard_map.127 = (f32[128,512]{1,0:T(8,128)S(1)}, bf16[512,128]{1,0:T(8,128)(2,1)}) custom-call(f32[128,512]{1,0:T(8,128)} %bitcast.20, s32[2,1,32]{2,1,0:T(1,128)} %bitcast.25, s32[2,4,32]{2,1,0:T(4,128)} %bitcast.23, bf16[2,4,32]{2,1,0:T(4,128)(2,1)} %bitcast.24, bf16[2,32]{1,0:T(2,128)(2,1)} %bitcast.26, bf16[64,128]{1,0:T(8,128)(2,1)} %bitcast.22), custom_call_target="tpu_custom_call" | custom-call | flops 10000000 | bytes 200000 | tf_op jit(solution)/shard_map/pallas_call | solution.py:407
  2.4 0.0 collective-permute-done.mate
  2.5 5.7 %collective-permute-start.1 = (bf16[144,512]{1,0:T(8,128)(2,1)S(1)}, bf16[144,512]{1,0:T(8,128)(2,1)S(1)}, u32[]{:S(2)}, u32[]{:S(2)}) collective-permute-start(bf16[144,512]{1,0:T(8,128)(2,1)S(1)} %shard_map.128), channel_id=1, source_target_pairs={{0,15},{1,2},{2,1},{3,4},{4,3},{5,6},{6,5},{7,8},{8,7},{9,10},{10,... | collective-permute-start | bytes 442376 | tf_op jit(solution)/shard_map/ppermute | solution.py:495
  8.2 3.5 %all-to-all-start = ((bf16[16,32,128]{2,1,0:T(8,128)(2,1)}), bf16[16,32,128]{2,1,0:T(8,128)(2,1)S(1)}, u32[]{:S(2)}, u32[]{:S(2)}) async-start(bf16[16,32,128]{2,1,0:T(8,128)(2,1)} %bitcast.12), calls=%async_computation | async-start | bytes 262144 | tf_op jit(solution)/shard_map/all_to_all | solution.py:496
  11.7 0.0 collective-permute-done.1.oth
  11.8 0.1 shard_map.129
  11.9 1.6 %collective-permute-start.3 = (f32[160,512]{1,0:T(8,128)S(1)}, f32[160,512]{1,0:T(8,128)S(1)}, u32[]{:S(2)}, u32[]{:S(2)}) collective-permute-start(f32[160,512]{1,0:T(8,128)S(1)} %get-tuple-element.29.control), channel_id=1, source_target_pairs={{16,0},{17,1},{18,2},{19,3},{20,4},{21,5},{22,6},{23,7},{24,8},{25... | collective-permute-start | bytes 983048 | tf_op jit(solution)/shard_map/ppermute | solution.py:461
  13.4 3.4 %shard_map.130 = (f32[64,512]{1,0:T(8,128)S(1)}, f32[192,512]{1,0:T(8,128)S(1)}, bf16[192,512]{1,0:T(8,128)(2,1)S(1)}, bf16[192,512]{1,0:T(8,128)(2,1)S(1)}, bf1...) custom-call(f32[1,512]{1,0:T(1,128)} %bitcast.28, bf16[512,512]{1,0:T(8,128)(2,1)} %ws_hbm.3, ...), custom_call_target="tpu_custom_call" | custom-call | flops 99999997952 | bytes 4000000 | tf_op jit(solution)/shard_map/pallas_call | solution.py:407
  16.9 0.6 %collective-permute-start.4 = (bf16[128,512]{1,0:T(8,128)(2,1)S(1)}, bf16[128,512]{1,0:T(8,128)(2,1)S(1)}, u32[]{:S(2)}, u32[]{:S(2)}) collective-permute-start(bf16[128,512]{1,0:T(8,128)(2,1)S(1)} %get-tuple-element.48), channel_id=1, source_target_pairs={{16,0},{17,1},{18,2},{19,3},{20,4},{21,5},{22,6},{23,7},{24,8},{25... | collective-permute-start | bytes 393224 | tf_op jit(solution)/shard_map/ppermute | solution.py:461
  17.5 2.2 %all-to-all-done = bf16[16,32,128]{2,1,0:T(8,128)(2,1)S(1)} async-done(((bf16[16,32,128]{2,1,0:T(8,128)(2,1)}), bf16[16,32,128]{2,1,0:T(8,128)(2,1)S(1)}, u32[]{:S(2)}, u32[]{:S(2)}) %all-to-all-start) | async-done | bytes 131104 | tf_op jit(solution)/shard_map/all_to_all | solution.py:496
  19.6 1.7 %shard_map.131 = (f32[192,512]{1,0:T(8,128)S(1)}, f32[192,512]{1,0:T(8,128)S(1)}, f32[128,128]{1,0:T(8,128)S(1)}, bf16[512,512]{1,0:T(8,128)(2,1)S(1)}, bf16[512...) custom-call(bf16[512,512]{1,0:T(8,128)(2,1)} %ws_hbm.3, ...), custom_call_target="tpu_custom_call" | custom-call | flops 1000000000 | bytes 2000000 | tf_op jit(solution)/shard_map/pallas_call | solution.py:407
  21.4 0.1 collective-permute-start.2
  21.5 1.2 %collective-permute-done.2.message = f32[128,128]{1,0:T(8,128)S(1)} collective-permute-done((f32[128,128]{1,0:T(8,128)S(1)}, f32[128,128]{1,0:T(8,128)S(1)}, u32[]{:S(2)}, u32[]{:S(2)}) %collective-permute-start.2) | collective-permute-done | bytes 65568 | tf_op jit(solution)/shard_map/ppermute | solution.py:532
  22.7 0.0 collective-permute-done.3.nxt
  22.7 1.7 %shard_map.132.base = f32[128,512]{1,0:T(8,128)S(1)} custom-call(f32[128,512]{1,0:T(8,128)S(1)} %get-tuple-element.32.control, f32[64,512]{1,0:T(8,128)S(1)} %get-tuple-element.33.edge0, f32[192,512]{1,0:T(8,128)S(1)} %get-tuple-element.34.u1x, bf16[192,512]{1,0:T(8,128)(2,1)S(1)} %get-tuple-element.35.d0x, bf16[192,512]{1,0:T(8,128)(2,1)S(1)} %get-tuple-element.36.d1x, ...), custom_call_target="tpu_custom_call" | custom-call | flops 603979776 | bytes 6000000 | tf_op jit(solution)/shard_map/pallas_call | solution.py:407
  24.4 0.3 %collective-permute-done.4.before = bf16[128,512]{1,0:T(8,128)(2,1)S(1)} collective-permute-done((bf16[128,512]{1,0:T(8,128)(2,1)S(1)}, bf16[128,512]{1,0:T(8,128)(2,1)S(1)}, u32[]{:S(2)}, u32[]{:S(2)}) %collective-permute-start.4) | collective-permute-done | bytes 131104 | tf_op jit(solution)/shard_map/ppermute | solution.py:461
  24.6 0.8 %shard_map.133 = f32[128,512]{1,0:T(8,128)} custom-call(f32[128,512]{1,0:T(8,128)S(1)} %shard_map.132.base, bf16[128,512]{1,0:T(8,128)(2,1)S(1)} %get-tuple-element.47.background, bf16[128,512]{1,0:T(8,128)(2,1)S(1)} %collective-permute-done.4.before, f32[1,512]{1,0:T(1,128)S(1)} %get-tuple-element.45.error), custom_call_target="tpu_custom_call" | custom-call | flops 1000000 | bytes 900000 | tf_op jit(solution)/shard_map/pallas_call | solution.py:407
  (1 shorter events, 0.0 us)
Async XLA Ops:
  0.0 2.4 %collective-permute-start = (f32[128,512]{1,0:T(8,128)}, f32[128,512]{1,0:T(8,128)S(1)}, u32[]{:S(2)}, u32[]{:S(2)}) collective-permute-start(f32[128,512]{1,0:T(8,128)} %bitcast.19), channel_id=1, source_target_pairs={{0,1},{1,0},{2,3},{3,2},{4,5},{5,4},{6,7},{7,6},{8,9},{9,8},{10,11... | collective-permute-start | bytes 786440 | tf_op jit(solution)/shard_map/ppermute | solution.py:464
  2.5 9.3 %collective-permute-start.1 = (bf16[144,512]{1,0:T(8,128)(2,1)S(1)}, bf16[144,512]{1,0:T(8,128)(2,1)S(1)}, u32[]{:S(2)}, u32[]{:S(2)}) collective-permute-start(bf16[144,512]{1,0:T(8,128)(2,1)S(1)} %shard_map.128), channel_id=1, source_target_pairs={{0,15},{1,2},{2,1},{3,4},{4,3},{5,6},{6,5},{7,8},{8,7},{9,10},{10,... | collective-permute-start | bytes 442376 | tf_op jit(solution)/shard_map/ppermute | solution.py:495
  8.2 11.4 %all-to-all-start = ((bf16[16,32,128]{2,1,0:T(8,128)(2,1)}), bf16[16,32,128]{2,1,0:T(8,128)(2,1)S(1)}, u32[]{:S(2)}, u32[]{:S(2)}) async-start(bf16[16,32,128]{2,1,0:T(8,128)(2,1)} %bitcast.12), calls=%async_computation | async-start | bytes 262144 | tf_op jit(solution)/shard_map/all_to_all | solution.py:496
  11.9 10.8 %collective-permute-start.3 = (f32[160,512]{1,0:T(8,128)S(1)}, f32[160,512]{1,0:T(8,128)S(1)}, u32[]{:S(2)}, u32[]{:S(2)}) collective-permute-start(f32[160,512]{1,0:T(8,128)S(1)} %get-tuple-element.29.control), channel_id=1, source_target_pairs={{16,0},{17,1},{18,2},{19,3},{20,4},{21,5},{22,6},{23,7},{24,8},{25... | collective-permute-start | bytes 983048 | tf_op jit(solution)/shard_map/ppermute | solution.py:461
  16.9 7.8 %collective-permute-start.4 = (bf16[128,512]{1,0:T(8,128)(2,1)S(1)}, bf16[128,512]{1,0:T(8,128)(2,1)S(1)}, u32[]{:S(2)}, u32[]{:S(2)}) collective-permute-start(bf16[128,512]{1,0:T(8,128)(2,1)S(1)} %get-tuple-element.48), channel_id=1, source_target_pairs={{16,0},{17,1},{18,2},{19,3},{20,4},{21,5},{22,6},{23,7},{24,8},{25... | collective-permute-start | bytes 393224 | tf_op jit(solution)/shard_map/ppermute | solution.py:461
  21.4 1.3 %collective-permute-start.2 = (f32[128,128]{1,0:T(8,128)S(1)}, f32[128,128]{1,0:T(8,128)S(1)}, u32[]{:S(2)}, u32[]{:S(2)}) collective-permute-start(f32[128,128]{1,0:T(8,128)S(1)} %get-tuple-element.40), channel_id=1, source_target_pairs={{0,1},{1,0},{2,3},{3,2},{4,5},{5,4},{6,7},{7,6},{8,9},{9,8},{10,11... | collective-permute-start | bytes 196616 | tf_op jit(solution)/shard_map/ppermute | solution.py:532

commit v2 on v1

--- a/solution.py
+++ b/solution.py
@@ -246,14 +246,11 @@
 
 def observe_kernel(
     tiles,
-    ws_hbm, wn_hbm, wo_hbm, readout_hbm, gain_hbm, error_hbm, control_hbm, background_hbm, arrived, field,
-    pull1, pull2, message, ws, wn, wo, readout, gain, error, control, background,
-    th, tl, ph, plo, vals, spread, wide, sems,
+    readout_hbm, error_hbm, wo_hbm, arrived, field,
+    spread, message, readout, error, wo,
+    th, tl, ph, plo, vals, wide, sems,
 ):
-    pairs = (
-        (readout_hbm, readout), (gain_hbm, gain), (error_hbm, error), (wo_hbm, wo), (wn_hbm, wn), (ws_hbm, ws),
-        (control_hbm, control), (background_hbm, background),
-    )
+    pairs = ((readout_hbm, readout), (error_hbm, error), (wo_hbm, wo))
     copies = [pltpu.make_async_copy(source, to, sems.at[i]) for i, (source, to) in enumerate(pairs)]
     for copy in copies:
         copy.start()
@@ -294,52 +291,32 @@
             start = (q * members + m) * 32
             value = mixed[q * 32 : (q + 1) * 32, m * LANES : (m + 1) * LANES] - target[q * 32 : (q + 1) * 32]
             spread[start : start + 32] = value.astype(BF16)
-    copies[0].wait()
-    pulled = dot_t(spread[...], readout[...])
     size = members * 32
-    row8 = sublane((8, 1))
-    for k, out in enumerate((pull1, pull2)):
-        own = k * size
-        away = (2 + k) * size
-        for r in range(2 * members):
-            out[r * SLIM : r * SLIM + 16] = pulled[own + r * 16 : own + (r + 1) * 16]
-            low = pulled[away + r * 16 : away + r * 16 + 8]
-            high = pulled[away + r * 16 + 8 : away + r * 16 + 16]
-            group = jnp.where(
-                even, jnp.where(row8 >= 4, high, 0.0), jnp.where(row8 < 4, low, 0.0)
-            )
-            out[r * SLIM + 16 : r * SLIM + 24] = group
-        for r in range(2 * members):
-            pair = spread[own + r * 16 : own + (r + 1) * 16].astype(F32)
-            near = jnp.where(even, pair[8:16], pair[0:8])
-            message[k * size // 2 + r * 8 : k * size // 2 + (r + 1) * 8] = near
-    for copy in copies[1:]:
+    for k in range(steps):
+        for m in range(members):
+            start = k * size + m * 32
+            pair = spread[start : start + 32].astype(F32)
+            near = [jnp.where(even, pair[i + 8 : i + 16], pair[i : i + 8]) for i in (0, 16)]
+            start = k * size // 2 + m * 16
+            message[start : start + 16] = jnp.concatenate(near, axis=0).astype(BF16)
+    for copy in copies:
         copy.wait()
 
 
-def adjoint_step(u, cot, gb, gm, flat, d, add, out, gain, ws, wn, wo, members):
-    both = 2 * SLIM
-    gb[...] = cot[...].astype(BF16)
-    flat[...] = dot_t(gb[...], wo[...])
-    gb[...] = (flat[...] * d[...]).astype(BF16)
-    gm[...] = dot_t(gb[...], wn[...])
-    flat[...] = dot_t(gb[...], ws[...])
+def finish_adjoint(u, parts, add, out, gain, members):
     for m in range(members):
-        base = m * both
-        rows = []
+        rows = [parts(2 * m + lat) for lat in range(2)]
+        around = neighbours([row[1].astype(BF16).astype(F32) for row in rows])
         for lat in range(2):
-            start = base + lat * SLIM
-            rows.append(gm[start : start + SLIM].astype(BF16).astype(F32))
-        around = neighbours(rows)
-        for lat in range(2):
-            start = base + lat * SLIM
+            r = 2 * m + lat
+            start = r * SLIM
             x = u[start : start + SLIM]
             s = inverse_rms(x)
-            scaled = gain * (flat[start : start + SLIM] + around[lat])
+            scaled = gain * (rows[lat][2] + around[lat])
             inner = jnp.mean(x * scaled, axis=-1, keepdims=True)
-            value = cot[start : start + SLIM] + s * scaled - x * (s * s * s * inner)
+            value = rows[lat][0] + s * scaled - x * (s * s * s * inner)
             if add is not None:
-                value = value + add[start : start + SLIM]
+                value = value + add(r)
             out[start : start + SLIM] = value
 
 
@@ -357,37 +334,105 @@
     return jnp.where(even, edge[0:8], edge[8:16])
 
 
-def backward_kernel(
-    control, edge0, u1x, d0x, d1x, f2x, pull1, pull2, message,
-    nxt, ws, wn, wo, gain, error, readout,
-    result,
-    cot, cot2, extra, gb, gm, flat, mate_pull, edge, u0x, final,
+def own_kernel(
+    wn_hbm, ws_hbm, spread, readout, error, wo, nxt, f2x, d1x,
+    cot_own, cot_edge, add_own, add_edge, gm_own, flat_own, wn, ws,
+    pulled, final, gb, edge, d, sems,
 ):
-    size = control.shape[0]
-    members = size // 32
+    pairs = ((wn_hbm, wn), (ws_hbm, ws))
+    copies = [pltpu.make_async_copy(source, to, sems.at[i]) for i, (source, to) in enumerate(pairs)]
+    for copy in copies:
+        copy.start()
+    size = cot_own.shape[0]
     even = lax.rem(lax.axis_index("tile"), 2) == 0
-    slot = lax.axis_index("slot")
-    later = jnp.where(slot == lax.axis_size("slot") - 1, 0.0, 1.0)
-    gain = gain[...]
+    later = jnp.where(lax.axis_index("slot") == lax.axis_size("slot") - 1, 0.0, 1.0)
     weight = later * error[...]
     row8 = sublane((8, 1))
-    mate_pull[...] = dot_t(message[...].astype(BF16), readout[...])
+    pulled[...] = dot_t(spread[...], readout[...])
+    final[...] = f2x[...].astype(F32)
+    d[...] = d1x[...].astype(F32)
+
+    def other_edge(k, r):
+        start = (2 + k) * size + r * 16
+        low = jnp.where(row8 < 4, pulled[start : start + 8], 0.0)
+        high = jnp.where(row8 >= 4, pulled[start + 8 : start + 16], 0.0)
+        return jnp.where(even, high, low)
+
+    for r in range(size // 16):
+        a, b = r * 16, (r + 1) * 16
+        at = r * SLIM
+        value = pulled[size + a : size + b] - weight * (nxt[a:b] - final[at : at + 16])
+        cot_own[a:b] = value
+        gb[a:b] = value.astype(BF16)
+        misfit = weight * (edges(nxt, size, edge, r) - final[at + 16 : at + 24])
+        cot_edge[r * 8 : (r + 1) * 8] = other_edge(1, r) - misfit
+        add_own[a:b] = pulled[a:b]
+        add_edge[r * 8 : (r + 1) * 8] = other_edge(0, r)
+    flat_own[...] = dot_t(gb[...], wo[...])
+    for r in range(size // 16):
+        a, b = r * 16, (r + 1) * 16
+        gb[a:b] = (flat_own[a:b] * d[r * SLIM : r * SLIM + 16]).astype(BF16)
+    copies[0].wait()
+    gm_own[...] = dot_t(gb[...], wn[...])
+    copies[1].wait()
+    flat_own[...] = dot_t(gb[...], ws[...])
+
+
+def backward_kernel(
+    gain_hbm, control_hbm, background_hbm, error, readout, wo, wn, ws, message, edge0, u1x, d0x, d1x,
+    cot_own, cot_edge, add_own, add_edge, gm_own, flat_own,
+    result, background,
+    cot, gb, gm, flat, mate_pull, u0x, d, gain, control, cot_all, add_all, gb_edge, gm_edge, flat_edge, sems,
+):
+    pairs = ((gain_hbm, gain), (control_hbm, control), (background_hbm, background))
+    copies = [pltpu.make_async_copy(source, to, sems.at[i]) for i, (source, to) in enumerate(pairs)]
+    for copy in copies:
+        copy.start()
+    size = result.shape[0]
+    members = size // 32
+    half = size // 2
+    even = lax.rem(lax.axis_index("tile"), 2) == 0
+    row8 = sublane((8, 1))
     mate_side = jnp.where(even, 1, 0) == jnp.where(row8 < 4, 1, 0)
-    final[...] = f2x[...].astype(F32)
+    mate_pull[...] = dot_t(message[...], readout[...])
+    d[...] = d1x[...].astype(F32)
     for r in range(2 * members):
-        a, b = r * SLIM, r * SLIM + 16
-        cot[a:b] = pull2[a:b] - weight * (nxt[r * 16 : (r + 1) * 16] - final[a:b])
-        c, e = b, b + 8
-        start = size // 2 + r * 8
-        pulled = pull2[c:e] + jnp.where(mate_side, mate_pull[start : start + 8], 0.0)
-        cot[c:e] = pulled - weight * (edges(nxt, size, edge, r) - final[c:e])
-        extra[a:b] = pull1[a:b]
-        extra[c:e] = pull1[c:e] + jnp.where(mate_side, mate_pull[r * 8 : (r + 1) * 8], 0.0)
-    adjoint_step(u1x, cot, gb, gm, flat, d1x, extra, cot2, gain, ws, wn, wo, members)
+        a, b = r * 8, (r + 1) * 8
+        cot_all[a:b] = cot_edge[a:b] + jnp.where(mate_side, mate_pull[half + a : half + b], 0.0)
+        add_all[a:b] = add_edge[a:b] + jnp.where(mate_side, mate_pull[a:b], 0.0)
+    gb_edge[...] = cot_all[...].astype(BF16)
+    gm_edge[...] = dot_t(gb_edge[...], wo[...])
+    for r in range(2 * members):
+        a, b = r * 8, (r + 1) * 8
+        gm_edge[a:b] = gm_edge[a:b] * d[r * SLIM + 16 : (r + 1) * SLIM]
+    gb_edge[...] = gm_edge[...].astype(BF16)
+    gm_edge[...] = dot_t(gb_edge[...], wn[...])
+    flat_edge[...] = dot_t(gb_edge[...], ws[...])
+
+    def joined(own, edge, r):
+        return jnp.concatenate([own[r * 16 : (r + 1) * 16], edge[r * 8 : (r + 1) * 8]], axis=0)
+
+    def first(r):
+        return joined(cot_own, cot_all, r), joined(gm_own, gm_edge, r), joined(flat_own, flat_edge, r)
+
+    copies[0].wait()
+    finish_adjoint(u1x, first, lambda r: joined(add_own, add_all, r), cot, gain[...], members)
+    for copy in copies[1:]:
+        copy.wait()
     for r in range(2 * members):
         u0x[r * SLIM : r * SLIM + 16] = control[r * 16 : (r + 1) * 16]
         u0x[r * SLIM + 16 : (r + 1) * SLIM] = edge0[r * 8 : (r + 1) * 8]
-    adjoint_step(u0x, cot2, gb, gm, flat, d0x, None, cot, gain, ws, wn, wo, members)
+    gb[...] = cot[...].astype(BF16)
+    flat[...] = dot_t(gb[...], wo[...])
+    gb[...] = (flat[...] * d0x[...].astype(F32)).astype(BF16)
+    gm[...] = dot_t(gb[...], wn[...])
+    flat[...] = dot_t(gb[...], ws[...])
+
+    def second(r):
+        at = slice(r * SLIM, (r + 1) * SLIM)
+        return cot[at], gm[at], flat[at]
+
+    finish_adjoint(u0x, second, None, cot, gain[...], members)
     for r in range(2 * members):
         a, b = r * 16, (r + 1) * 16
         result[a:b] = cot[r * SLIM : r * SLIM + 16] + error[...] * control[a:b]
@@ -515,30 +560,41 @@
     )(gain, self_weight, neighbour_weight, output_weight, readout, message, near4, oth)
     before = across(final, -1, straight)
     total = -(-tiles // SENDERS) * LANES
-    handed = [self_weight, neighbour_weight, output_weight, readout, gain, error]
-    handed += [flat, background.reshape(size, channels)]
-    pull1, pull2, message, *handed = kernel_call(
+    spread, near_spread, readout_held, error_held, wo = kernel_call(
         functools.partial(observe_kernel, tiles),
-        [spec(slim), spec(slim), spec(size, F32, LANES)]
-        + [jax.ShapeDtypeStruct(block.shape, block.dtype) for block in handed],
+        [spec(4 * size, BF16, LANES), spec(size, BF16, LANES)]
+        + [spec(channels, BF16, LANES), spec(1), spec(channels, BF16)],
         [scratch(128, BF16, total)] * 4
-        + [scratch(total, F32, LANES), scratch(4 * size, BF16, LANES), scratch(tiles * CHUNK, F32, LANES)]
-        + [pltpu.SemaphoreType.DMA((8,))],
+        + [scratch(total, F32, LANES), scratch(tiles * CHUNK, F32, LANES), pltpu.SemaphoreType.DMA((3,))],
         10**9,
         2000000,
-        hbm=8,
-    )(*handed, arrived, field)
-    ws, wn, wo, readout, gain, error, held, background = handed
-    from_mate = lax.ppermute(message, "tile", mate_of)
-    base = kernel_call(
+        hbm=3,
+    )(readout, error, output_weight, arrived, field)
+    from_mate = lax.ppermute(near_spread, "tile", mate_of)
+    *own, wn, ws = kernel_call(
+        own_kernel,
+        [spec(size), spec(size // 2), spec(size), spec(size // 2), spec(size), spec(size)]
+        + [spec(channels, BF16), spec(channels, BF16)],
+        [scratch(4 * size), scratch(slim), scratch(size, BF16), scratch(16), scratch(slim)]
+        + [pltpu.SemaphoreType.DMA((2,))],
+        10**9,
+        3000000,
+        hbm=2,
+    )(neighbour_weight, self_weight, spread, readout_held, error_held, wo, nxt, f2x, d1x)
+    base, background_held = kernel_call(
         backward_kernel,
-        spec(size),
-        [scratch(slim), scratch(slim), scratch(slim), scratch(slim, BF16), scratch(slim), scratch(slim)]
-        + [scratch(size), scratch(16), scratch(slim), scratch(slim)],
+        [spec(size), spec(size, BF16)],
+        [scratch(slim), scratch(slim, BF16), scratch(slim), scratch(slim), scratch(size), scratch(slim)]
+        + [scratch(slim), scratch(1), scratch(size), scratch(size // 2), scratch(size // 2)]
+        + [scratch(size // 2, BF16), scratch(size // 2), scratch(size // 2), pltpu.SemaphoreType.DMA((3,))],
         12 * slim * channels * channels,
         6000000,
-    )(held, edge0, u1x, d0x, d1x, f2x, pull1, pull2, from_mate, nxt, ws, wn, wo, gain, error, readout)
-    result = kernel_call(last_kernel, spec(size), [], 10**6, 900000)(base, background, before, error)
+        hbm=3,
+    )(
+        gain, flat, background.reshape(size, channels), error_held, readout_held, wo, wn, ws, from_mate,
+        edge0, u1x, d0x, d1x, *own,
+    )
+    result = kernel_call(last_kernel, spec(size), [], 10**6, 900000)(base, background_held, before, error_held)
     return result.reshape(control.shape)
 
 

time: 25.7 us -> 27.3 us (1.062)
  Pallas kernels: 9.69 us -> 11.2 us
    pallas_call x7 -> x8, Pallas kernels: 9.69 us -> 11.2 us  [call(): pl.pallas_call(body, out_shape=outs, in_specs=[pl.BlockSpec(memory_space=...]
    ppermute x2, waiting for transfers between devices: 0.27 us -> 1.58 us  [across(): return lax.ppermute(block, ('slot', 'tile'), pairs)]
    ppermute x1, waiting for transfers between devices: 1.24 us -> 0.01 us  [per_device(): from_mate = lax.ppermute(near_spread, 'tile', mate_of)]
  transfers between devices with their start and end apart: 6 -> 6, of which waited for: 3 -> 2; matrix products, arithmetic and copies ran while one was open for 0% -> 0% of each run, Pallas kernels for 35% -> 38%
where the time goes in v2:
time: 27.3 us; the launch traced here: 27 us
  starting transfers between devices  11.9 us (44%)
  Pallas kernels  11.2 us (41%)
  waiting for transfers between devices  3.77 us (14%)
    pallas_call x8, Pallas kernels, call(): pl.pallas_call(body, out_shape=outs, in_specs=[pl.BlockSpec(memory_space=...  11.2 us
    ppermute x1, starting transfers between devices, per_device(): oth = lax.ppermute(sent, 'tile', other_of)  5.73 us
    all_to_all x1, starting transfers between devices, per_device(): lax.all_to_all(packed, 'tile', split_axis=0, concat_axis=0, tiled=True)  3.51 us
    all_to_all x1, waiting for transfers between devices, per_device(): lax.all_to_all(packed, 'tile', split_axis=0, concat_axis=0, tiled=True)  2.19 us
    ppermute x2, starting transfers between devices, across(): return lax.ppermute(block, ('slot', 'tile'), pairs)  2.16 us
    ppermute x2, waiting for transfers between devices, across(): return lax.ppermute(block, ('slot', 'tile'), pairs)  1.58 us
  transfers between devices with their start and end apart: 6, of which 2 were waited for; matrix products, arithmetic and copies ran while one was open for 0% of the time, Pallas kernels for 38%

profile of v2, /device:TPU:0, one launch (start us, length us, event | category | flops | bytes accessed | tf_op | source)
XLA Modules:
  0.0 27.0 jit_solution(16707659848820938896)
XLA Ops:
  0.0 0.5 %collective-permute-start = (f32[128,512]{1,0:T(8,128)}, f32[128,512]{1,0:T(8,128)S(1)}, u32[]{:S(2)}, u32[]{:S(2)}) collective-permute-start(f32[128,512]{1,0:T(8,128)} %bitcast.19), channel_id=1, source_target_pairs={{0,1},{1,0},{2,3},{3,2},{4,5},{5,4},{6,7},{7,6},{8,9},{9,8},{10,11... | collective-permute-start | bytes 786440 | tf_op jit(solution)/shard_map/ppermute | solution.py:509
  0.5 2.0 %shard_map.127 = (f32[128,512]{1,0:T(8,128)S(1)}, bf16[512,128]{1,0:T(8,128)(2,1)}) custom-call(f32[128,512]{1,0:T(8,128)} %bitcast.20, s32[2,1,32]{2,1,0:T(1,128)} %bitcast.28, s32[2,4,32]{2,1,0:T(4,128)} %bitcast.24, bf16[2,4,32]{2,1,0:T(4,128)(2,1)} %bitcast.27, bf16[2,32]{1,0:T(2,128)(2,1)} %bitcast.29, bf16[64,128]{1,0:T(8,128)(2,1)} %bitcast.23), custom_call_target="tpu_custom_call" | custom-call | flops 10000000 | bytes 200000 | tf_op jit(solution)/shard_map/pallas_call | solution.py:452
  2.4 0.0 collective-permute-done.mate
  2.5 5.7 %collective-permute-start.1 = (bf16[144,512]{1,0:T(8,128)(2,1)S(1)}, bf16[144,512]{1,0:T(8,128)(2,1)S(1)}, u32[]{:S(2)}, u32[]{:S(2)}) collective-permute-start(bf16[144,512]{1,0:T(8,128)(2,1)S(1)} %shard_map.128), channel_id=1, source_target_pairs={{0,15},{1,2},{2,1},{3,4},{4,3},{5,6},{6,5},{7,8},{8,7},{9,10},{10,... | collective-permute-start | bytes 442376 | tf_op jit(solution)/shard_map/ppermute | solution.py:540
  8.2 3.5 %all-to-all-start = ((bf16[16,32,128]{2,1,0:T(8,128)(2,1)}), bf16[16,32,128]{2,1,0:T(8,128)(2,1)S(1)}, u32[]{:S(2)}, u32[]{:S(2)}) async-start(bf16[16,32,128]{2,1,0:T(8,128)(2,1)} %bitcast.12), calls=%async_computation | async-start | bytes 262144 | tf_op jit(solution)/shard_map/all_to_all | solution.py:541
  11.7 0.0 collective-permute-done.1.oth
  11.8 0.1 shard_map.129
  11.9 1.6 %collective-permute-start.2 = (f32[160,512]{1,0:T(8,128)S(1)}, f32[160,512]{1,0:T(8,128)S(1)}, u32[]{:S(2)}, u32[]{:S(2)}) collective-permute-start(f32[160,512]{1,0:T(8,128)S(1)} %get-tuple-element.33.control), channel_id=1, source_target_pairs={{16,0},{17,1},{18,2},{19,3},{20,4},{21,5},{22,6},{23,7},{24,8},{25... | collective-permute-start | bytes 983048 | tf_op jit(solution)/shard_map/ppermute | solution.py:506
  13.4 3.4 %shard_map.130 = (f32[64,512]{1,0:T(8,128)S(1)}, f32[192,512]{1,0:T(8,128)S(1)}, bf16[192,512]{1,0:T(8,128)(2,1)S(1)}, bf16[192,512]{1,0:T(8,128)(2,1)S(1)}, bf1...) custom-call(f32[1,512]{1,0:T(1,128)} %bitcast.25, bf16[512,512]{1,0:T(8,128)(2,1)} %ws_hbm.3, ...), custom_call_target="tpu_custom_call" | custom-call | flops 99999997952 | bytes 4000000 | tf_op jit(solution)/shard_map/pallas_call | solution.py:452
  16.9 0.6 %collective-permute-start.4 = (bf16[128,512]{1,0:T(8,128)(2,1)S(1)}, bf16[128,512]{1,0:T(8,128)(2,1)S(1)}, u32[]{:S(2)}, u32[]{:S(2)}) collective-permute-start(bf16[128,512]{1,0:T(8,128)(2,1)S(1)} %get-tuple-element.56), channel_id=1, source_target_pairs={{16,0},{17,1},{18,2},{19,3},{20,4},{21,5},{22,6},{23,7},{24,8},{25... | collective-permute-start | bytes 393224 | tf_op jit(solution)/shard_map/ppermute | solution.py:506
  17.5 2.2 %all-to-all-done = bf16[16,32,128]{2,1,0:T(8,128)(2,1)S(1)} async-done(((bf16[16,32,128]{2,1,0:T(8,128)(2,1)}), bf16[16,32,128]{2,1,0:T(8,128)(2,1)S(1)}, u32[]{:S(2)}, u32[]{:S(2)}) %all-to-all-start) | async-done | bytes 131104 | tf_op jit(solution)/shard_map/all_to_all | solution.py:541
  19.6 1.2 %shard_map.131 = (bf16[512,128]{1,0:T(8,128)(2,1)S(1)}, bf16[128,128]{1,0:T(8,128)(2,1)S(1)}, bf16[512,128]{1,0:T(8,128)(2,1)S(1)}, f32[1,512]{1,0:T(1,128)S(1)}, bf16[512,512]{1,0:T(8,128)(2,1)S(1)}) custom-call(bf16[512,128]{1,0:T(8,128)(2,1)} %readout_hbm.3, f32[1,512]{1,0:T(1,128)} %bitcast.30, bf16[512,512]{1,0:T(8,128)(2,1)} %wo_hbm.3, ...), custom_call_target="tpu_custom_call" | custom-call | flops 1000000000 | bytes 2000000 | tf_op jit(solution)/shard_map/pallas_call | solution.py:452
  20.8 0.1 collective-permute-start.3
  20.9 1.6 %collective-permute-done.2.nxt = f32[160,512]{1,0:T(8,128)S(1)} collective-permute-done((f32[160,512]{1,0:T(8,128)S(1)}, f32[160,512]{1,0:T(8,128)S(1)}, u32[]{:S(2)}, u32[]{:S(2)}) %collective-permute-start.2) | collective-permute-done | bytes 327712 | tf_op jit(solution)/shard_map/ppermute | solution.py:506
  22.5 1.7 %shard_map.132 = (f32[128,512]{1,0:T(8,128)S(1)}, f32[64,512]{1,0:T(8,128)S(1)}, f32[128,512]{1,0:T(8,128)S(1)}, f32[64,512]{1,0:T(8,128)S(1)}, f32[128,512]{1,0...) custom-call(bf16[512,512]{1,0:T(8,128)(2,1)} %wn_hbm.3, ...), custom_call_target="tpu_custom_call" | custom-call | flops 1000000000 | bytes 3000000 | tf_op jit(solution)/shard_map/pallas_call | solution.py:452
  24.2 0.0 collective-permute-done.3.message
  24.2 2.0 %shard_map.133 = (f32[128,512]{1,0:T(8,128)S(1)}, bf16[128,512]{1,0:T(8,128)(2,1)S(1)}) custom-call(f32[1,512]{1,0:T(1,128)} %bitcast.26, f32[128,512]{1,0:T(8,128)} %bitcast.21, bf16[128,512]{1,0:T(8,128)(2,1)} %bitcast.22, f32[1,512]{1,0:T(1,128)S(1)} %get-tuple-element.36.error, bf16[512,128]{1,0:T(8,128)(2,1)S(1)} %get-tuple-element.37.readout, ...), custom_call_target="tpu_custom_call" | custom-call | flops 603979776 | bytes 6000000 | tf_op jit(solution)/shard_map/pallas_call | solution.py:452
  26.2 0.0 collective-permute-done.4.before
  26.2 0.8 %shard_map.134 = f32[128,512]{1,0:T(8,128)} custom-call(f32[128,512]{1,0:T(8,128)S(1)} %get-tuple-element.54.base, bf16[128,512]{1,0:T(8,128)(2,1)S(1)} %get-tuple-element.55.background, bf16[128,512]{1,0:T(8,128)(2,1)S(1)} %collective-permute-done.4.before, f32[1,512]{1,0:T(1,128)S(1)} %get-tuple-element.36.error), custom_call_target="tpu_custom_call" | custom-call | flops 1000000 | bytes 900000 | tf_op jit(solution)/shard_map/pallas_call | solution.py:452
  (1 shorter events, 0.0 us)
Async XLA Ops:
  0.0 2.4 %collective-permute-start = (f32[128,512]{1,0:T(8,128)}, f32[128,512]{1,0:T(8,128)S(1)}, u32[]{:S(2)}, u32[]{:S(2)}) collective-permute-start(f32[128,512]{1,0:T(8,128)} %bitcast.19), channel_id=1, source_target_pairs={{0,1},{1,0},{2,3},{3,2},{4,5},{5,4},{6,7},{7,6},{8,9},{9,8},{10,11... | collective-permute-start | bytes 786440 | tf_op jit(solution)/shard_map/ppermute | solution.py:509
  2.5 9.3 %collective-permute-start.1 = (bf16[144,512]{1,0:T(8,128)(2,1)S(1)}, bf16[144,512]{1,0:T(8,128)(2,1)S(1)}, u32[]{:S(2)}, u32[]{:S(2)}) collective-permute-start(bf16[144,512]{1,0:T(8,128)(2,1)S(1)} %shard_map.128), channel_id=1, source_target_pairs={{0,15},{1,2},{2,1},{3,4},{4,3},{5,6},{6,5},{7,8},{8,7},{9,10},{10,... | collective-permute-start | bytes 442376 | tf_op jit(solution)/shard_map/ppermute | solution.py:540
  8.2 11.4 %all-to-all-start = ((bf16[16,32,128]{2,1,0:T(8,128)(2,1)}), bf16[16,32,128]{2,1,0:T(8,128)(2,1)S(1)}, u32[]{:S(2)}, u32[]{:S(2)}) async-start(bf16[16,32,128]{2,1,0:T(8,128)(2,1)} %bitcast.12), calls=%async_computation | async-start | bytes 262144 | tf_op jit(solution)/shard_map/all_to_all | solution.py:541
  11.9 10.6 %collective-permute-start.2 = (f32[160,512]{1,0:T(8,128)S(1)}, f32[160,512]{1,0:T(8,128)S(1)}, u32[]{:S(2)}, u32[]{:S(2)}) collective-permute-start(f32[160,512]{1,0:T(8,128)S(1)} %get-tuple-element.33.control), channel_id=1, source_target_pairs={{16,0},{17,1},{18,2},{19,3},{20,4},{21,5},{22,6},{23,7},{24,8},{25... | collective-permute-start | bytes 983048 | tf_op jit(solution)/shard_map/ppermute | solution.py:506
  16.9 9.4 %collective-permute-start.4 = (bf16[128,512]{1,0:T(8,128)(2,1)S(1)}, bf16[128,512]{1,0:T(8,128)(2,1)S(1)}, u32[]{:S(2)}, u32[]{:S(2)}) collective-permute-start(bf16[128,512]{1,0:T(8,128)(2,1)S(1)} %get-tuple-element.56), channel_id=1, source_target_pairs={{16,0},{17,1},{18,2},{19,3},{20,4},{21,5},{22,6},{23,7},{24,8},{25... | collective-permute-start | bytes 393224 | tf_op jit(solution)/shard_map/ppermute | solution.py:506
  20.8 3.3 %collective-permute-start.3 = (bf16[128,128]{1,0:T(8,128)(2,1)S(1)}, bf16[128,128]{1,0:T(8,128)(2,1)S(1)}, u32[]{:S(2)}, u32[]{:S(2)}) collective-permute-start(bf16[128,128]{1,0:T(8,128)(2,1)S(1)} %get-tuple-element.44), channel_id=1, source_target_pairs={{0,1},{1,0},{2,3},{3,2},{4,5},{5,4},{6,7},{7,6},{8,9},{9,8},{10,11... | collective-permute-start | bytes 98312 | tf_op jit(solution)/shard_map/ppermute | solution.py:573
